TPU v7x, 32 devices: a whole 2x2x4 slice. The times are simulated.
32 devices in a mesh: section: 2 (over x), tensor: 4 (over y, core), dp: 4 (over z).
Axes of the slice: x: 2, y: 2, z: 4, core: 2. Of those that a mesh axis runs over, the one named last changes fastest.
Arguments:
- images: bfloat16 [8, 256, 1152], P('dp', 'tensor'), may hold values from -6 to 6
- timesteps: int32 [8], P('dp'), may hold values from 0 to 999
- t_table: bfloat16 [1000, 1152], replicated, may hold values from -6 to 6
- rel_index: int32 [256, 256], replicated, may hold values from 0 to 960, as said below
- w_qkv: bfloat16 [2, 1152, 3, 1152], P('section', None, None, 'tensor'), may hold values from -0.1875 to 0.1875
- w_time: bfloat16 [2, 1152, 3, 1152], P('section', None, None, 'tensor'), may hold values from -0.1875 to 0.1875
- w_out: bfloat16 [2, 1152, 1152], P('section', 'tensor'), may hold values from -0.5 to 0.5
- w_fc1: bfloat16 [2, 1152, 4608], P('section', None, 'tensor'), may hold values from -0.1875 to 0.1875
- w_fc2: bfloat16 [2, 4608, 1152], P('section', 'tensor'), may hold values from -0.09375 to 0.09375
- rel_table: float32 [2, 961, 16], P('section', None, 'tensor'), may hold values from -4 to 4
- norm_gain: float32 [2, 2, 1152], P('section'), may hold values from 0.1 to 1.9
- norm_shift: float32 [2, 2, 1152], P('section'), may hold values from -2 to 2
- cotangent: bfloat16 [8, 256, 1152], P('dp', 'tensor'), may hold values from -6 to 6
Outputs:
- output: bfloat16 [8, 256, 1152], P('dp', 'tensor')
- input_grads: bfloat16 [2, 8, 256, 1152], P('section', 'dp', 'tensor')
- g_qkv: float32 [2, 1152, 3, 1152], P('section', 'dp', None, 'tensor')
- g_time: float32 [2, 1152, 3, 1152], P('section', 'dp', None, 'tensor')
- g_out: float32 [2, 1152, 1152], P('section', 'tensor', 'dp')
- g_fc1: float32 [2, 1152, 4608], P('section', 'dp', 'tensor')
- g_fc2: float32 [2, 4608, 1152], P('section', 'tensor', 'dp')
- g_table: float32 [2, 961, 16], P('section', None, 'tensor')
- g_gain: float32 [2, 2, 1152], P('section')
- g_shift: float32 [2, 2, 1152], P('section')
Inputs may be any that keep to these rules, and one draw needn't show every extreme that they name: `rel_index`: tokens at the same offset between rows and between columns of the patch grid share a bucket; every bucket is used.
All inputs are finite; a program needn't handle non-finite values.
Results may differ from a plain program's by a relative error of at most 0.02.
Values may be sent and summed in bfloat16 or wider, within the bound.
A program may use at most 256 MiB of HBM per device.

v0:
```python
import functools

import jax
import jax.numpy as jnp
from jax import lax
from jax.experimental import pallas as pl
from jax.experimental.pallas import tpu as pltpu
from jax.sharding import PartitionSpec as P

MESH = pl.DeviceIdType.MESH
F32 = jnp.float32
BF16 = jnp.bfloat16
EPS = 1e-06
GELU_A = 0.7978845608028654
GELU_B = 0.044715
ATT, MLP, DMLP, DATT = range(4)
slot_of = (0, 1, 0, 0)


def mm(a, b):
    return lax.dot_general(a, b, (((1,), (0,)), ((), ())), preferred_element_type=F32)


def mm_nt(a, b):
    return lax.dot_general(a, b, (((1,), (1,)), ((), ())), preferred_element_type=F32)


def mm_tn(a, b):
    return lax.dot_general(a, b, (((0,), (0,)), ((), ())), preferred_element_type=F32)


def gelu_parts(v):
    square = v * v
    th = jnp.tanh(v * (GELU_A + (GELU_A * GELU_B) * square))
    up = 0.5 + 0.5 * th
    slope = up + v * (1.0 - th * th) * (0.5 * GELU_A + (1.5 * GELU_A * GELU_B) * square)
    return v * up, slope


def head_windows(heads, local):
    width = local // heads
    found = []
    for h in range(heads):
        lo = h * width // 128 * 128
        hi = min(-(-(h + 1) * width // 128) * 128, local)
        found.append((lo, hi, h * width - lo, (h + 1) * width - lo))
    return found


def only(x, start, stop):
    lane = lax.broadcasted_iota(jnp.int32, x.shape, 1)
    return jnp.where((lane >= start) & (lane < stop), x, jnp.zeros_like(x))


def in_thirds(x):
    high = x.astype(BF16)
    rest = x - high.astype(F32)
    middle = rest.astype(BF16)
    low = (rest - middle.astype(F32)).astype(BF16)
    return jnp.concatenate([high, middle, low], axis=0)


def add_thirds(x):
    rows = x.shape[0] // 3
    return x[:rows] + x[rows : 2 * rows] + x[2 * rows :]


def wider(x, lanes):
    return jnp.concatenate([x, jnp.zeros((x.shape[0], lanes - x.shape[1]), x.dtype)], axis=1)


def block_kernel(
    cfg,
    x_hbm, cot_hbm, wq_hbm, wt_hbm, wo_hbm, w1_hbm, w2_hbm, temb_hbm, gain_hbm, shift_hbm, rel_hbm, tab_hbm,
    out_hbm, ig_hbm, parts_ref, g2_hbm, g1_hbm, gq_hbm, go_hbm, gt_hbm, gtab_hbm, ggain_hbm, gshift_hbm,
    temb_ref, gain_ref, shift_ref, rel_ref, tab_ref, out_ref, ig_ref, tot_ref, mlp_ref, stage, tok_ref, emb_ref,
    gtab_ref, small_ref, ggain_ref, gshift_ref,
    wq_ref, wo_ref, w1_ref, w2_ref, tp_ref, tx_ref, chosen, tab, partial, sums, arrived,
    tiny_s, small_r,
    xin, mid, gath, keep, rcv_c, rcv_y, snd_c, snd_y, bias, prob, qkv, att, act, dgel,
    xhat, inv, ymid, dy1, dqkv, dtail, dh, acc, turned, line, far_att, dqkv2, dtail2, far_att2,
    load_s, store_s, ag_s, ag_r, rs_s, rs_r, sec_s, sec_r, ch_s, ch_r, fac_s, fac_r, li_s, li_r, ti_s, ti_r, sm_s, sm_r,
):
    count, rows, seq, heads, ring, chained = cfg
    half_rows = 2 * rows
    wide = -(-wo_ref.shape[0] // 128) * 128
    width = x_hbm.shape[-1]
    local = wo_ref.shape[0]
    grid = int(round(seq**0.5))
    windows = head_windows(heads, local)
    scale = (local // heads) ** (-0.5)
    blocks = 4
    cut = width // blocks
    pieces = sums.shape[0]
    slim = cut // pieces
    full = dqkv.shape[0]
    lanes = full * dqkv.shape[-1] + dtail.shape[-1]

    s = lax.axis_index("section")
    t = lax.axis_index("tensor")
    z = lax.axis_index("dp")
    core = t + 1 - 2 * (t % 2)
    far = (t + 2) % 4
    fcore = (core + 2) % 4
    here = t // 2
    there = 1 - here
    own = pl.ds(pl.multiple_of(t * rows, rows), rows)

    wt_ref = partial.at[0, : 3 * local, :]

    loads = [
        pltpu.make_async_copy(src, dst, load_s.at[n])
        for n, (src, dst) in enumerate(
            (
                (wt_hbm, wt_ref), (wq_hbm, wq_ref), (wo_hbm, wo_ref), (w1_hbm, w1_ref), (w2_hbm, w2_ref),
                (temb_hbm, temb_ref), (gain_hbm, gain_ref), (shift_hbm, shift_ref), (rel_hbm, rel_ref),
                (tab_hbm, tab_ref),
            )
        )
    ]
    first_rows = pltpu.make_async_copy(x_hbm, xin, load_s.at[10])
    last_rows = pltpu.make_async_copy(cot_hbm, xin, load_s.at[11])

    def cot_rows(i):
        return pltpu.make_async_copy(cot_hbm.at[i], gath.at[DMLP, i, own, :], load_s.at[12 + i])

    @pl.when(s == 0)
    def _():
        first_rows.start()

    @pl.when(s == 1)
    def _():
        for i in range(count):
            cot_rows(i).start()

    for load in loads[5:] + loads[:5]:
        load.start()

    barrier = pltpu.get_barrier_semaphore()
    for peer in ({"tensor": core}, {"tensor": far}, {"tensor": fcore}, {"section": 1 - s}):
        pl.semaphore_signal(barrier, inc=1, device_id=peer, device_id_type=MESH)

    def greet(j, carry):
        pl.semaphore_signal(barrier, inc=1, device_id={"dp": (z + j) % ring}, device_id_type=MESH)
        return carry

    lax.fori_loop(1, ring, greet, 0)

    def rows_of(owner):
        return pl.ds(pl.multiple_of(owner * rows, rows), rows)

    def half_of(half):
        return pl.ds(pl.multiple_of(half * half_rows, half_rows), half_rows)

    def ag_copy(k, i, which):
        owner, to = ((t, core), (t, far), (far, core))[which]
        ref = gath.at[k % 3, i, rows_of(owner), :]
        return pltpu.make_async_remote_copy(
            src_ref=ref, dst_ref=ref, send_sem=ag_s.at[k, i, which], recv_sem=ag_r.at[k, i, which],
            device_id={"tensor": to}, device_id_type=MESH,
        )

    def ag_start(k, i):
        ag_copy(k, i, 1).start()
        ag_copy(k, i, 0).start()

    def ag_near(k, i):
        ag_copy(k, i, 0).wait_recv()

    def ag_pass(k, i):
        ag_copy(k, i, 1).wait_recv()
        ag_copy(k, i, 2).start()

    def ag_rest(k, i):
        ag_copy(k, i, 2).wait_recv()

    def ag_done(k, i):
        for which in range(3):
            ag_copy(k, i, which).wait_send()

    def rs_copy(k, i, which):
        if which < 2:
            src, dst, to = snd_c.at[slot_of[k], i, which], rcv_c.at[slot_of[k], i, which], core
        else:
            src, dst, to = snd_y.at[slot_of[k], i], rcv_y.at[slot_of[k], i], far
        return pltpu.make_async_remote_copy(
            src_ref=src, dst_ref=dst, send_sem=rs_s.at[k, i, which], recv_sem=rs_r.at[k, i, which],
            device_id={"tensor": to}, device_id_type=MESH,
        )

    def rs_give(k, i, which, part):
        odd = t % 2 == 1
        low, high = part[:rows], part[rows:]
        snd_c[slot_of[k], i, which] = jnp.where(odd, low, high).astype(BF16)
        rs_copy(k, i, which).start()
        keep[slot_of[k], i, which] = jnp.where(odd, high, low)

    def rs_pass(k, i):
        rs_copy(k, i, 0).wait_recv()
        snd_y[slot_of[k], i] = (keep[slot_of[k], i, 0] + rcv_c[slot_of[k], i, 0].astype(F32)).astype(BF16)
        rs_copy(k, i, 2).start()

    def rs_take(k, i):
        rs_copy(k, i, 1).wait_recv()
        near = keep[slot_of[k], i, 1] + rcv_c[slot_of[k], i, 1].astype(F32)
        rs_copy(k, i, 2).wait_recv()
        return near + rcv_y[slot_of[k], i].astype(F32)

    def rs_done(k, i):
        for which in range(3):
            rs_copy(k, i, which).wait_send()

    def sec_copy(j, src, dst):
        return lambda i: pltpu.make_async_remote_copy(
            src_ref=src.at[i], dst_ref=dst.at[i], send_sem=sec_s.at[j, i], recv_sem=sec_r.at[j, i],
            device_id={"section": 1 - s}, device_id_type=MESH,
        )

    mid_copy = sec_copy(0, mid, xin)
    grad_copy = sec_copy(1, ig_ref, xin)
    out_copy = sec_copy(2, out_ref, out_ref)

    def tiny_copy(n, j):
        ref = (emb_ref, tok_ref)[n]
        return pltpu.make_async_remote_copy(
            src_ref=ref.at[z], dst_ref=ref.at[z], send_sem=ti_s.at[n, j], recv_sem=ti_r.at[n, j],
            device_id={"dp": (z + j) % ring}, device_id_type=MESH,
        )

    def over_ring(body):
        def run(j, carry):
            body(j)
            return carry

        lax.fori_loop(1, ring, run, 0)

    def small_copy(n, j):
        return pltpu.make_async_remote_copy(
            src_ref=tiny_s.at[n], dst_ref=small_r.at[n, j], send_sem=sm_s.at[n, j], recv_sem=sm_r.at[n, j],
            device_id={"tensor": (core, far, fcore)[j]}, device_id_type=MESH,
        )

    mate = z + 1 - 2 * (z % 2)
    across = 3 - z
    beyond = 3 * (2 - z)
    is_end = (z == 0) | (z == 3)
    is_mate = (z == 1) | (z == 2)
    base = z * count if chained else 0
    place = {ATT: (turned, 0), DATT: (turned, 1), MLP: (line, 0), DMLP: (line, 1)}

    def block(b):
        return pl.ds(pl.multiple_of(b * cut, cut), cut)

    def factor_copy(n):
        if n < 2:
            src, dst = turned.at[n, t % 2], turned.at[n, count + t % 2]
        else:
            pairs = [(dqkv.at[c], dqkv2.at[c]) for c in range(full)] + [(dtail, dtail2), (far_att, far_att2)]
            src, dst = pairs[n - 2]
        return pltpu.make_async_remote_copy(
            src_ref=src, dst_ref=dst, send_sem=fac_s.at[n], recv_sem=fac_r.at[n],
            device_id={"dp": mate}, device_id_type=MESH,
        )

    def share_copy(k):
        ref = turned.at[k, count + t % 2]
        return pltpu.make_async_remote_copy(
            src_ref=ref, dst_ref=ref, send_sem=fac_s.at[4 + full + k], recv_sem=fac_r.at[4 + full + k],
            device_id={"tensor": core}, device_id_type=MESH,
        )

    def give_factor(*which):
        if chained:

            @pl.when(is_end)
            def _():
                for n in which:
                    factor_copy(n).start()

    def share_factor(k):
        if chained:

            @pl.when(is_mate)
            def _():
                factor_copy(k).wait_recv()
                share_copy(k).start()

    def cross_copy(slot, c):
        return pltpu.make_async_remote_copy(
            src_ref=sums.at[c, block((beyond, across)[slot]), :], dst_ref=arrived.at[slot, c],
            send_sem=ch_s.at[slot, c], recv_sem=ch_r.at[slot, c],
            device_id={"dp": across}, device_id_type=MESH,
        )

    def home_copy(c):
        return pltpu.make_async_remote_copy(
            src_ref=sums.at[c, block(mate), :], dst_ref=arrived.at[0, c],
            send_sem=ch_s.at[2, c], recv_sem=ch_r.at[0, c],
            device_id={"dp": mate}, device_id_type=MESH,
        )

    def rest_product(c, at, side):
        def by(n, right):
            return sum(mm(turned[n, side * count + i, at, :], right[i]) for i in range(count))

        if c < full:
            return by(0, (dqkv, dqkv2)[side].at[c])
        return wider(by(0, (dtail, dtail2)[side]), wide) + by(1, (far_att, far_att2)[side])

    def own_rest():
        @pl.when(is_end)
        def _():
            for c in range(full + 1):
                sums[c, block(z), :] = rest_product(c, block(z), 0).astype(BF16)

        @pl.when(is_mate)
        def _():
            def half(h, carry):
                at = pl.ds(pl.multiple_of(h * 2 * cut, 2 * cut), 2 * cut)
                for c in range(full + 1):
                    sums[c, at, :] = rest_product(c, at, 0).astype(BF16)
                return carry

            lax.fori_loop(0, 2, half, 0)

    def give_rest(c):
        def add(b):
            both_sides = sums[c, block(b), :].astype(F32) + rest_product(c, block(b), 1)
            sums[c, block(b), :] = both_sides.astype(BF16)

        @pl.when(is_mate)
        def _():
            if c < full:
                factor_copy(2 + c).wait_recv()
            else:
                share_copy(0).wait_recv()
                share_copy(1).wait_recv()
                factor_copy(2 + full).wait_recv()
                factor_copy(3 + full).wait_recv()
            add(beyond)
            cross_copy(0, c).start()
            if c < full:
                cross_copy(1, full if c == 0 else c - 1).start()
            add(across)
            if c == full - 1:
                cross_copy(1, c).start()
            add(z)

    def relay(c):
        @pl.when(is_mate)
        def _():
            cross_copy(0, c).wait_recv()
            home = sums[c, block(mate), :].astype(F32) + arrived[0, c].astype(F32)
            sums[c, block(mate), :] = home.astype(BF16)
            home_copy(c).start()

    def settle(c):
        def finish(slot, copy):
            copy.wait_recv()
            whole = sums[c, block(z), :].astype(F32) + arrived[slot, c].astype(F32)
            tot_ref[:, c * wide : (c + 1) * wide] = whole.astype(BF16)

        @pl.when(is_mate)
        def _():
            finish(1, cross_copy(1, c))

        @pl.when(is_end)
        def _():
            finish(0, home_copy(c))

    def weights_left():
        @pl.when(is_end)
        def _():
            for n in range(4 + full):
                factor_copy(n).wait_send()

        @pl.when(is_mate)
        def _():
            for k in range(2):
                share_copy(k).wait_send()
            for c in range(pieces):
                cross_copy(0, c).wait_send()
                cross_copy(1, c).wait_send()
                home_copy(c).wait_send()

        for n in range(2):
            for right in (True, False):

                @pl.when(z < ring - 1 if right else z > 0)
                def _():
                    line_copy(n, z, right).wait_send()

                for d in range(1, ring):
                    zs, there_is = upstream(d, right)

                    @pl.when(there_is)
                    def _():
                        line_share(n, zs).wait_send()

                        @pl.when(z < ring - 1 if right else z > 0)
                        def _():
                            line_copy(n, zs, right).wait_send()

    def line_copy(n, zs, right):
        ref = line.at[n, zs * count + t % 2]
        way = 0 if right else 1
        return pltpu.make_async_remote_copy(
            src_ref=ref, dst_ref=ref, send_sem=li_s.at[n, way, zs], recv_sem=li_r.at[n, way, zs],
            device_id={"dp": (z + 1) % ring if right else (z + ring - 1) % ring}, device_id_type=MESH,
        )

    def line_share(n, zs):
        ref = line.at[n, zs * count + t % 2]
        return pltpu.make_async_remote_copy(
            src_ref=ref, dst_ref=ref, send_sem=li_s.at[n, 2, zs], recv_sem=li_r.at[n, 2, zs],
            device_id={"tensor": core}, device_id_type=MESH,
        )

    def upstream(d, right):
        return (z - d, z >= d) if right else (z + d, z + d < ring)

    def line_start(n):
        if chained:
            for right in (True, False):

                @pl.when(z < ring - 1 if right else z > 0)
                def _():
                    line_copy(n, z, right).start()

    def line_pass(n, d):
        for right in (True, False) if chained else ():
            zs, there_is = upstream(d, right)

            @pl.when(there_is)
            def _():
                line_copy(n, zs, right).wait_recv()

                @pl.when(z < ring - 1 if right else z > 0)
                def _():
                    line_copy(n, zs, right).start()

                line_share(n, zs).start()

    def mlp_own():
        at = pl.ds(pl.multiple_of(z * cut, cut), cut)
        for m, n, right in ((0, 1, act), (1, 0, dh)):
            mlp_ref[m] = sum(mm(line[n, base + i, at, :], right[i]) for i in range(count))

    def mlp_of(zs):
        at = pl.ds(pl.multiple_of(z * cut, cut), cut)
        for n in range(2):
            line_share(n, zs).wait_recv()

        def step(j, carry):
            slot = zs * count + j // pieces
            cols = pl.ds(pl.multiple_of(j % pieces * (width // pieces), 128), width // pieces)
            v = mm(partial[0, cols, :], line[0, slot])
            value, slope = gelu_parts(v)
            back = (mm(w2_ref[cols, :], line[1, slot]) * slope).astype(BF16)
            mlp_ref[0, :, cols] += mm_nt(line[1, slot, at, :], value.astype(BF16))
            mlp_ref[1, :, cols] += mm_nt(line[0, slot, at, :], back)
            return carry

        lax.fori_loop(0, count * pieces, step, 0)

    def turn_image(k, i):
        ref, n = place[k]
        ref[n, base + i if ref is line else i] = gath[k % 3, i].T

    def turn(k):
        for i in range(count):
            turn_image(k, i)

    def each_image(body):
        def run(i, carry):
            body(i)
            return carry

        lax.fori_loop(0, count, run, 0)

    def norm(x, which, i):
        mean = jnp.mean(x, axis=-1, keepdims=True)
        centre = x - mean
        root = lax.rsqrt(jnp.mean(centre * centre, axis=-1, keepdims=True) + EPS)
        hat = centre * root
        xhat[which, i] = hat
        inv[which, i] = jnp.broadcast_to(root, (rows, 128))
        return (hat * gain_ref[which : which + 1, :] + shift_ref[which : which + 1, :]).astype(BF16)

    def norm_back(da, which, i):
        hat = xhat[which, i]
        tiny_s[0, which : which + 1, :] += jnp.sum(da * hat, axis=0, keepdims=True)
        tiny_s[0, 2 + which : 3 + which, :] += jnp.sum(da, axis=0, keepdims=True)
        dhat = da * gain_ref[which : which + 1, :]
        m1 = jnp.mean(dhat, axis=-1, keepdims=True)
        m2 = jnp.mean(dhat * hat, axis=-1, keepdims=True)
        return inv[which, i][:, :1] * (dhat - m1 - hat * m2)

    def turn_qkv():
        loads[1].wait()
        for r in range(0, width, wide):
            for c in range(3):
                partial[1, r : r + wide, c * wide : c * wide + local] = wq_ref[
                    c * local : (c + 1) * local, r : r + wide
                ].T

    def turn_weight(to, ref):
        for r in range(0, width, wide):
            to[r : r + wide, : ref.shape[0]] = ref[:, r : r + wide].T

    def lead(k, end, near):
        def first(i):
            end(i)

            @pl.when(i == count - 1)
            def _():
                ag_pass(k, 0)

            ag_near(k, i)
            near(i)

        each_image(first)

    def follow(k, rest):
        def second(i):
            ag_rest(k, i)
            rest(i)

            @pl.when(i < count - 1)
            def _():
                ag_pass(k, i + 1)

            rs_pass(k, i)

        each_image(second)

    tiny_s[...] = jnp.zeros_like(tiny_s)
    tok_ref[z] = jnp.zeros_like(tok_ref[z])
    emb_ref[z] = jnp.zeros_like(emb_ref[z])
    for load in loads[5:]:
        load.wait()
    emb_ref[z, :count, :] = temb_ref[...].astype(F32)

    def norm_input(i):
        gath[ATT, i, own, :] = norm(xin[i].astype(F32), 0, i)

    @pl.when(s == 0)
    def _():
        first_rows.wait()
        each_image(norm_input)

    pl.semaphore_wait(barrier, 3 + ring)
    over_ring(lambda j: tiny_copy(0, j).start())

    @pl.when(s == 1)
    def _():
        def begin(i):
            cot_rows(i).wait()
            ag_start(DMLP, i)

        each_image(begin)

    def take_input(i):
        mid_copy(i).wait_recv()
        norm_input(i)
        ag_start(ATT, i)

    lane = lax.broadcasted_iota(jnp.int32, (1, 2 * seq), 1)

    def tables():
        valid = lane < (2 * grid - 1) * grid
        slab = pltpu.roll(wider(rel_ref[:grid, :], 2 * seq), grid * (grid - 1), 1)
        for k in range(grid - 1):
            r = grid - 1 - k
            block = only(rel_ref[r * grid : (r + 1) * grid, :128], 0, grid)
            slab += pltpu.roll(wider(block, 2 * seq), k * grid, 1)
        none = jnp.full((1, 2 * seq), -1, jnp.int32)
        before = none
        for c in range(1, grid):
            moved = pltpu.roll(slab[c : c + 1, :], grid - c, 1)
            before = jnp.where((lane % grid == grid - c) & valid, moved, before)
        order = jnp.concatenate([jnp.where(valid, slab[:1, :], none), before], axis=1)
        step = 128
        for r in range(0, chosen.shape[0], step):
            bucket = r + lax.broadcasted_iota(jnp.int32, (step, 4 * seq), 0)
            chosen[r : r + step, :] = jnp.where(bucket == order, 1.0, 0.0).astype(BF16)
        tab[...] = jnp.zeros_like(tab)
        tab[:heads, : tab_ref.shape[1]] = tab_ref[...]
        found = add_thirds(mm(in_thirds(tab[...]), chosen[...]))
        after, before = found[:, : 2 * seq], found[:, 2 * seq :]
        for c in range(grid):
            low = pltpu.roll(after, c, 1) if c else after
            high = pltpu.roll(before, 2 * seq - (grid - c), 1)
            row = jnp.where(lane % grid >= c, low, high)
            for h in range(heads):
                tx_ref[h, c : c + 1, :] = row[h : h + 1, :]

        def expand(h, carry):
            for r in range(grid):
                shift = (2 * seq - grid * (grid - 1 - r)) % (2 * seq)
                bias[h, r * grid : (r + 1) * grid, :] = pltpu.roll(tx_ref[h], shift, 1)[:, :seq]
            return carry

        lax.fori_loop(0, heads, expand, 0)
        loads[0].wait()
        tp_ref[...] = jnp.zeros_like(tp_ref)
        emb = jnp.concatenate([temb_ref[...], jnp.zeros((16 - count, width), BF16)], axis=0)
        for c in range(3):
            tp_ref[c] = mm_nt(emb, partial[0, c * local : (c + 1) * local, :])

    @pl.when(s == 1)
    def _():
        tables()

        def spread_cot(i):
            ag_pass(DMLP, i)
            ag_near(DMLP, i)
            ag_rest(DMLP, i)

        each_image(spread_cot)
        turn(DMLP)
        line_start(1)
        turn_qkv()
        loads[2].wait()
        turn_weight(sums.at[0], wo_ref)
        loads[3].wait()
        turn_weight(partial.at[0], w1_ref)
        loads[4].wait()

        def early(i):
            dh[i] = mm_nt(gath[DMLP, i], w2_ref[...]).astype(BF16)

        each_image(early)
        line_pass(1, 1)

    @pl.when(s == 0)
    def _():
        each_image(lambda i: ag_start(ATT, i))
        tables()
        turn_qkv()
        for n in (2, 3, 4):
            loads[n].wait()

    def project(i, half):
        a = gath[ATT, i, half_of(half), :]
        part = mm(a, partial[1, :, : 2 * wide + local])
        for c in range(3):
            qkv[c, i, half_of(half), :] = (
                part[:, c * wide : c * wide + local] + tp_ref[c, pl.ds(i, 1), :]
            ).astype(BF16)

    def att_first(i):
        @pl.when(s == 1)
        def _():
            take_input(i)

    lead(ATT, att_first, lambda i: project(i, here))

    def att_rest(i):
        project(i, there)
        acc[0] = jnp.zeros_like(acc[0])
        for h, (lo, hi, start, stop) in enumerate(windows):
            q = only(qkv[0, i, :, lo:hi], start, stop)
            scores = mm_nt(q, qkv[1, i, :, lo:hi]) * scale + bias[h]
            top = jnp.max(scores, axis=-1, keepdims=True)
            expo = jnp.exp(scores - top)
            p = expo * (1.0 / jnp.sum(expo, axis=-1, keepdims=True))
            p = p.astype(BF16)
            prob[i, h] = p
            acc[0, :, lo:hi] += mm(p, only(qkv[2, i, :, lo:hi], start, stop))
        att[i] = acc[0, :, :local].astype(BF16)
        far_att[i] = pltpu.roll(acc[0], far_att.shape[-1] - local, 1).astype(BF16)
        rs_give(ATT, i, 0, mm(att[i, half_of(there), :], wo_ref[...]))
        rs_give(ATT, i, 1, mm(att[i, half_of(here), :], wo_ref[...]))

    follow(ATT, att_rest)

    turn(ATT)
    give_factor(0, 3 + full)

    def att_end(i):
        y = xin[i].astype(F32) + rs_take(ATT, i)
        ag_done(ATT, i)
        rs_done(ATT, i)
        ymid[i] = y
        gath[MLP, i, own, :] = norm(y, 1, i)
        ag_start(MLP, i)

    def mlp_half(i, half, which):
        a = gath[MLP, i, half_of(half), :]
        v = mm(a, w1_ref[...])
        value, slope = gelu_parts(v)
        act[i, half_of(half), :] = value.astype(BF16)
        dgel[i, half_of(half), :] = slope.astype(BF16)
        rs_give(MLP, i, which, mm(act[i, half_of(half), :], w2_ref[...]))

    def mlp_end(i):
        y = (ymid[i] + rs_take(MLP, i)).astype(BF16)
        rs_done(MLP, i)

        @pl.when(s == 0)
        def _():
            mid[i] = y
            mid_copy(i).start()

        @pl.when(s == 1)
        def _():
            out_ref[i] = y
            out_copy(i).start()

    def take_grad(i):
        mid_copy(i).wait_send()
        grad_copy(i).wait_recv()
        gath[DMLP, i, own, :] = xin[i]
        ag_start(DMLP, i)

    def dmlp_half(i, half, which):
        @pl.when(s == 0)
        def _():
            dh[i, half_of(half), :] = mm(gath[DMLP, i, half_of(half), :], partial[1]).astype(BF16)

        dact = dh[i, half_of(half), :].astype(F32)
        dh[i, half_of(half), :] = (dact * dgel[i, half_of(half), :].astype(F32)).astype(BF16)
        rs_give(DMLP, i, which, mm(dh[i, half_of(half), :], partial[0]))

    def mlp_rest(i):
        ag_rest(MLP, i)
        mlp_half(i, there, 0)

        @pl.when(i < count - 1)
        def _():
            ag_pass(MLP, i + 1)

        @pl.when(s == 0)
        def _():
            rs_pass(MLP, i)

        @pl.when(s == 1)
        def _():
            dmlp_half(i, there, 0)
            dmlp_half(i, here, 1)
            rs_pass(DMLP, i)

    lead(MLP, att_end, lambda i: mlp_half(i, here, 1))
    each_image(mlp_rest)
    turn(MLP)
    line_start(0)

    def dmlp_rest(i):
        @pl.when(i == count - 1)
        def _():
            turn(DMLP)
            line_start(1)

        dmlp_half(i, there, 0)

    @pl.when(s == 0)
    def _():
        each_image(mlp_end)
        turn_weight(partial.at[0], w1_ref)
        turn_weight(partial.at[1], w2_ref)
        turn_weight(sums.at[0], wo_ref)
        for d in range(1, ring):
            line_pass(0, d)
        lead(DMLP, take_grad, lambda i: dmlp_half(i, here, 1))
        follow(DMLP, dmlp_rest)

    @pl.when(s == 1)
    def _():
        last_rows.start()
        last_rows.wait()

    def dmlp_end(i):
        grad = xin[i].astype(F32) + norm_back(rs_take(DMLP, i), 1, i)
        rs_done(DMLP, i)
        dy1[i] = grad
        gath[DATT % 3, i, own, :] = grad.astype(BF16)
        ag_start(DATT, i)

    def datt_part(i, half):
        att[i, half_of(half), :] = mm(
            gath[DATT % 3, i, half_of(half), :], sums[0, :, :local]
        ).astype(BF16)

    def turn_factor(i):
        turn_image(DATT, i)

        @pl.when(i == t % 2)
        def _():
            give_factor(1)

    lead(DATT, dmlp_end, lambda i: datt_part(i, here))

    @pl.when(s == 0)
    def _():
        line_pass(1, 1)

        def gathered(i):
            ag_rest(DATT, i)
            turn_factor(i)

            @pl.when(i < count - 1)
            def _():
                ag_pass(DATT, i + 1)

        each_image(gathered)

    def datt_rest(i):
        @pl.when(s == 1)
        def _():
            ag_rest(DATT, i)

        datt_part(i, there)

        @pl.when(s == 1)
        def _():
            turn_factor(i)

        acc[...] = jnp.zeros_like(acc)
        for h, (lo, hi, start, stop) in enumerate(windows):
            q = only(qkv[0, i, :, lo:hi], start, stop)
            k = only(qkv[1, i, :, lo:hi], start, stop)
            d = only(att[i, :, lo:hi], start, stop)
            low = prob[i, h]
            p = low.astype(F32)
            dp = mm_nt(d, qkv[2, i, :, lo:hi])
            inner = jnp.sum(p * dp, axis=-1, keepdims=True)
            ds = (p * (dp - inner)).astype(BF16)

            @pl.when(i == 0)
            def _():
                bias[h] = ds.astype(F32)

            @pl.when(i > 0)
            def _():
                bias[h] += ds.astype(F32)

            acc[0, :, lo:hi] += mm(ds, k)
            acc[1, :, lo:hi] += mm_tn(ds, q)
            acc[2, :, lo:hi] += mm_tn(low, d)
        tiles = [None] * (lanes // 128)
        for c, by in enumerate((scale, scale, 1.0)):
            first = c * local // 128
            moved = acc[c] * by
            if c * local > first * 128:
                moved = pltpu.roll(moved, c * local - first * 128, 1)
            for n in range(moved.shape[1] // 128):
                tile = moved[:, n * 128 : (n + 1) * 128]
                tiles[first + n] = tile if tiles[first + n] is None else tiles[first + n] + tile
        per = wide // 128
        over_tokens = []
        for c in range(full + 1):
            part = jnp.concatenate(tiles[c * per : (c + 1) * per], axis=1).astype(BF16)
            if c < full:
                dqkv[c, i] = part
            else:
                dtail[i] = part
            over_tokens.append(jnp.sum(part.astype(F32), axis=0, keepdims=True))
        tok_ref[z, pl.ds(i, 1), :lanes] = jnp.concatenate(over_tokens, axis=1)
        last = 3 * local - full * wide
        for which, half in ((0, there), (1, here)):
            da = mm(dtail[i, half_of(half), :last], wq_ref[full * wide :, :])
            for c in range(full):
                da += mm(dqkv[c, i, half_of(half), :], wq_ref[c * wide : (c + 1) * wide, :])
            rs_give(DATT, i, which, da)

        @pl.when((s == 1) & (i < count - 1))
        def _():
            ag_pass(DATT, i + 1)

        rs_pass(DATT, i)

    each_image(datt_rest)

    give_factor(2 + full, *range(2, 2 + full))

    @pl.when(s == 1)
    def _():
        line_pass(0, 1)

    def first_parts():
        own_rest()
        mlp_own()
        share_factor(0)
        share_factor(1)

    ig_store = pltpu.make_async_copy(ig_ref, ig_hbm, store_s.at[18])
    out_store = pltpu.make_async_copy(out_ref, out_hbm, store_s.at[19])

    def end_of_chain(r, carry):
        if chained:
            pl.when(r == s)(first_parts)

        @pl.when(r == 0)
        def _():
            line_pass(1, 2)

        @pl.when(r == 1)
        def _():
            line_pass(0, 2)

        if chained:

            @pl.when(r == s)
            def _():
                give_rest(full)

        @pl.when(r == 0)
        def _():

            def datt_end(i):
                grad = dy1[i] + norm_back(rs_take(DATT, i), 0, i)
                ig_ref[i] = grad.astype(BF16)

                @pl.when(s == 1)
                def _():
                    grad_copy(i).start()

            each_image(datt_end)

            ig_store.start()

            @pl.when(s == 0)
            def _():
                each_image(lambda i: out_copy(i).wait_recv())
                out_store.start()

            @pl.when(s == 1)
            def _():
                each_image(lambda i: rs_pass(MLP, i))

            for j in range(3):
                small_copy(0, j).start()

            def fold(h, carry):
                total = jnp.zeros((grid, 2 * seq), F32)
                for r in range(grid):
                    part = wider(bias[h, r * grid : (r + 1) * grid, :], 2 * seq)
                    shift = grid * (grid - 1 - r)
                    total += part if shift == 0 else pltpu.roll(part, shift, 1)
                after = total[:1, :]
                before = jnp.zeros((1, 2 * seq), F32)
                for c in range(1, grid):
                    row = total[c : c + 1, :]
                    late = lane % grid >= c
                    after += pltpu.roll(jnp.where(late, row, 0.0), 2 * seq - c, 1)
                    before += pltpu.roll(jnp.where(late, 0.0, row), grid - c, 1)
                tok_ref[z, pl.ds(count + h, 1), : 4 * seq] = jnp.concatenate([after, before], axis=1)
                return carry

            lax.fori_loop(0, heads, fold, 0)
            for j in range(3):
                small_copy(0, j).wait_recv()
            over_tensor = tiny_s[0] + small_r[0, 0] + small_r[0, 1] + small_r[0, 2]
            row = lax.broadcasted_iota(jnp.int32, over_tensor.shape, 0)
            tok_ref[z, count + heads : count + heads + 1, :] = jnp.sum(
                jnp.where(row == t, over_tensor, 0.0), axis=0, keepdims=True
            )
            over_ring(lambda j: tiny_copy(1, j).start())

            @pl.when(s == 1)
            def _():
                each_image(mlp_end)
                out_store.start()

        return carry

    lax.fori_loop(0, 1 + s, end_of_chain, 0)

    if chained:
        give_rest(0)

        def others(j, carry):
            d = 1 + j // 2
            zs = z - d + 2 * d * (j % 2)

            @pl.when((zs >= 0) & (zs < ring))
            def _():
                mlp_of(zs)

            @pl.when(j == 0)
            def _():
                for c in range(1, full):
                    give_rest(c)
                relay(full)
                relay(0)

            @pl.when(j == 1)
            def _():
                for c in range(1, full):
                    relay(c)

            @pl.when((j == 3) & (s == 1))
            def _():
                line_pass(0, 3)

            @pl.when(j == 3)
            def _():
                line_pass(1, 3)

            return carry

        lax.fori_loop(0, 2 * (ring - 1), others, 0)
    else:

        def whole(b, carry):
            at = block(b)
            parts_ref[0, b] = sum(mm(line[1, i, at, :], act[i]) for i in range(count)).astype(BF16)
            parts_ref[1, b] = sum(mm(line[0, i, at, :], dh[i]) for i in range(count)).astype(BF16)
            parts_ref[2, b] = jnp.concatenate(
                [rest_product(c, at, 0) for c in range(full + 1)], axis=1
            ).astype(BF16)
            return carry

        lax.fori_loop(0, blocks, whole, 0)
    stores = []

    def store(src, dst):
        copy = pltpu.make_async_copy(src, dst, store_s.at[len(stores)])
        copy.start()
        stores.append(copy)
        return copy

    mlp_stores = []
    if chained:
        mlp_stores = [store(mlp_ref.at[0], g2_hbm), store(mlp_ref.at[1], g1_hbm)]
    over_ring(lambda j: tiny_copy(1, j).wait_recv())

    def add_slot(j, total):
        return total + tok_ref[j]

    total = lax.fori_loop(0, ring, add_slot, jnp.zeros(tok_ref.shape[1:], F32))
    tiny_s[1] = total
    for j in range(3):
        small_copy(1, j).start()
    tab[...] = jnp.zeros_like(tab)
    tab[:heads, :] = tiny_s[1, count : count + heads, : 4 * seq]
    found = add_thirds(mm_nt(in_thirds(tab[...]), chosen[...]))
    gtab_ref[...] = found[:heads, : gtab_ref.shape[1]]
    store(gtab_ref, gtab_hbm)

    over_ring(lambda j: tiny_copy(0, j).wait_recv())
    mine = width // ring
    tall = gt_hbm.shape[1]
    rows_of_emb = emb_ref[...].reshape(ring * 8, width)
    rows_of_emb = pltpu.roll(rows_of_emb, (width - z * mine) % width, 1)[:, :mine].astype(BF16)
    right = in_thirds(tok_ref[...].reshape(ring * 8, width)[:, :lanes])
    over_images = mm_tn(jnp.concatenate([rows_of_emb] * 3, axis=0), right)
    for copy in mlp_stores:
        copy.wait()
    room = mlp_ref.at[0] if chained else stage
    time_stores = []
    for c in range(3):
        first = c * local // 128 * 128
        window = over_images[:, first : first + wide]
        if c * local > first:
            window = pltpu.roll(window, wide - (c * local - first), 1)
        room[:mine, c * wide : (c + 1) * wide] = window
        time_stores.append(store(room.at[pl.ds(0, tall), pl.ds(c * wide, wide)], gt_hbm.at[c]))
    if chained:
        for c in (full, *range(full)):
            settle(c)
        for c in range(3):
            first = c * local // 128 * 128
            window = tot_ref[:, first : first + wide].astype(F32)
            if c * local > first:
                window = pltpu.roll(window, wide - (c * local - first), 1)
            mlp_ref[1, :, c * wide : (c + 1) * wide] = window
            store(mlp_ref.at[1, :, pl.ds(c * wide, wide)], gq_hbm.at[c])
        window = tot_ref[:, width - wide :].astype(F32)
        window = pltpu.roll(window, wide - (3 * local - (width - wide)), 1)
        for copy in time_stores:
            copy.wait()
        mlp_ref[0, :, :wide] = wider(window.T[:local], wide)
        store(mlp_ref.at[0, :, pl.ds(0, wide)], go_hbm)
    for j in range(3):
        small_copy(1, j).wait_recv()
    last = count + heads
    small_ref[pl.ds(t, 1), :] = tiny_s[1, last : last + 1, :]
    for j, owner in enumerate((core, far, fcore)):
        small_ref[pl.ds(owner, 1), :] = small_r[1, j, last : last + 1, :]
    ggain_ref[...] = small_ref[:2, :]
    gshift_ref[...] = small_ref[2:, :]
    store(ggain_ref, ggain_hbm)
    store(gshift_ref, gshift_hbm)

    def finish(i):
        for k in (MLP, DMLP, DATT):
            ag_done(k, i)
        rs_done(DATT, i)

        @pl.when(s == 1)
        def _():
            out_copy(i).wait_send()
            grad_copy(i).wait_send()

    each_image(finish)
    ig_store.wait()
    out_store.wait()

    def tiny_left(j):
        tiny_copy(0, j).wait_send()
        tiny_copy(1, j).wait_send()

    over_ring(tiny_left)
    for j in range(3):
        small_copy(0, j).wait_send()
        small_copy(1, j).wait_send()
    if chained:
        weights_left()
    waited = mlp_stores + (time_stores if chained else [])
    for copy in stores:
        if all(copy is not done for done in waited):
            copy.wait()


def run_block(x, cot, wq, wt, wo, w1, w2, temb, gain, shift, rel, table, ring):
    count, rows, width = x.shape
    seq = rel.shape[0]
    heads = table.shape[0]
    local = wo.shape[0]
    hidden = w1.shape[1]
    chained = ring == 4 and count == 2 and width % (16 * ring) == 0
    blocks = 4
    pieces = 3 if width // 4 % 48 == 0 else 1
    cut = width // blocks
    padded = -(-local // 128) * 128
    lanes = -(-3 * local // 128) * 128
    dims = (count, rows, seq, heads, ring, chained)
    full = 3 * local // padded
    assert pieces == full + 1 and padded * pieces == width
    mine = width // ring
    small = (8, 128)
    out_shape = [
        jax.ShapeDtypeStruct((count, rows, width), BF16),
        jax.ShapeDtypeStruct((count, rows, width), BF16),
        jax.ShapeDtypeStruct((16, 128) if chained else (3, blocks, cut, width), BF16),
        jax.ShapeDtypeStruct((cut, width) if chained else small, F32),
        jax.ShapeDtypeStruct((cut, width) if chained else small, F32),
        jax.ShapeDtypeStruct((3, cut, padded) if chained else small, F32),
        jax.ShapeDtypeStruct((local, padded) if chained else small, F32),
        jax.ShapeDtypeStruct((3, -(-mine // 8) * 8, padded), F32),
        jax.ShapeDtypeStruct(table.shape, F32),
        jax.ShapeDtypeStruct((2, width), F32),
        jax.ShapeDtypeStruct((2, width), F32),
    ]
    vm = pltpu.VMEM
    dma = pltpu.SemaphoreType.DMA
    scratch = [
        vm(temb.shape, BF16),
        vm(gain.shape, F32),
        vm(shift.shape, F32),
        vm(rel.shape, jnp.int32),
        vm(table.shape, F32),
        vm((count, rows, width), BF16),
        vm((count, rows, width), BF16),
        vm((cut, width) if chained else (16, 128), BF16),
        vm((2, cut, width) if chained else (2, 8, 128), F32),
        vm(small if chained else (-(-mine // 8) * 8, 3 * padded), F32),
        vm((ring, 8, width), F32),
        vm((ring, 8, width), F32),
        vm(table.shape, F32),
        vm((4, width), F32),
        vm((2, width), F32),
        vm((2, width), F32),
        vm(wq.shape, BF16),
        vm(wo.shape, BF16),
        vm(w1.shape, BF16),
        vm(w2.shape, BF16),
        vm((3, 16, local), F32),
        vm((heads, int(round(seq**0.5)), 2 * seq), F32),
        vm((4 * seq, 4 * seq), BF16),
        vm((16, 4 * seq), F32),
        vm((2, width, width), BF16),
        vm((pieces, width, padded), BF16),
        vm((2, pieces, cut, padded) if chained else (16, 128), BF16),
        vm((2, 8, width), F32),
        vm((2, 3, 8, width), F32),
        vm((count, rows, width), BF16),
        vm((count, rows, width), BF16),
        vm((3, count, seq, width), BF16),
        vm((2, count, 2, rows, width), F32),
        vm((2, count, 2, rows, width), BF16),
        vm((2, count, rows, width), BF16),
        vm((2, count, 2, rows, width), BF16),
        vm((2, count, rows, width), BF16),
        vm((heads, seq, seq), F32),
        vm((count, heads, seq, seq), BF16),
        vm((3, count, seq, local), BF16),
        vm((count, seq, local), BF16),
        vm((count, seq, hidden), BF16),
        vm((count, seq, hidden), BF16),
        vm((2, count, rows, width), F32),
        vm((2, count, rows, 128), F32),
        vm((count, rows, width), F32),
        vm((count, rows, width), F32),
        vm((full, count, seq, padded), BF16),
        vm((count, seq, lanes - full * padded), BF16),
        vm((count, seq, hidden), BF16),
        vm((3, seq, padded), F32),
        vm((2, 2 * count if chained else count, width, seq), BF16),
        vm((2, ring * count if chained else count, width, seq), BF16),
        vm((count, seq, padded), BF16),
        vm((full, count, seq, padded) if chained else (16, 128), BF16),
        vm((count, seq, lanes - full * padded) if chained else (16, 128), BF16),
        vm((count, seq, padded) if chained else (16, 128), BF16),
        dma((12 + count,)),
        dma((20,)),
        dma((4, count, 3)),
        dma((4, count, 3)),
        dma((4, count, 3)),
        dma((4, count, 3)),
        dma((3, count)),
        dma((3, count)),
        dma((3, pieces)),
        dma((2, pieces)),
        dma((6 + full,)),
        dma((6 + full,)),
        dma((2, 3, ring)),
        dma((2, 3, ring)),
        dma((2, ring)),
        dma((2, ring)),
        dma((2, 3)),
        dma((2, 3)),
    ]
    whole = pl.BlockSpec(memory_space=pltpu.VMEM)
    lies = pl.BlockSpec(memory_space=pl.ANY)
    return pl.pallas_call(
        functools.partial(block_kernel, dims),
        out_shape=out_shape,
        in_specs=[lies] * 12,
        out_specs=[lies] * 2 + [lies if chained else whole] + [lies] * 8,
        scratch_shapes=scratch,
        compiler_params=pltpu.CompilerParams(
            collective_id=0, has_side_effects=True, vmem_limit_bytes=63 * 2**20
        ),
        name="blocks",
    )(x, cot, wq, wt, wo, w1, w2, temb, gain, shift, rel, table)


def per_device(
    images, timesteps, t_table, rel_index, w_qkv, w_time, w_out, w_fc1, w_fc2, rel_table,
    norm_gain, norm_shift, cotangent,
):
    ring = lax.axis_size("dp")
    count = images.shape[0]
    width = images.shape[-1]
    local = w_out.shape[1]
    cut = width // ring
    embedded = jnp.concatenate(
        [lax.dynamic_slice_in_dim(t_table, timesteps[i], 1, axis=0) for i in range(count)], axis=0
    )
    wq = jnp.transpose(w_qkv[0], (1, 2, 0)).reshape(3 * local, width)
    wt = jnp.transpose(w_time[0], (1, 2, 0)).reshape(3 * local, width)
    output, in_grad, parts, g_fc2, g_fc1, g_qkv, g_out, g_time, g_table, g_gain, g_shift = run_block(
        images, cotangent, wq, wt, w_out[0], w_fc1[0], w_fc2[0], embedded, norm_gain[0], norm_shift[0],
        rel_index, rel_table[0].T, ring,
    )
    if parts.ndim == 4:
        parts = lax.psum_scatter(
            parts.reshape(3, width, width), "dp", scatter_dimension=1, tiled=True
        ).astype(F32)
        g_fc2, g_fc1, rest = parts
        g_qkv = jnp.transpose(rest[:, : 3 * local].reshape(cut, 3, local), (1, 0, 2))
        g_out = rest[:, 3 * local :].T
    else:
        g_qkv, g_out = g_qkv[:, :, :local], g_out[:, :cut]
    g_time = g_time[:, : width // ring, :local]
    return (
        output, in_grad[None], jnp.transpose(g_qkv, (1, 0, 2))[None], jnp.transpose(g_time, (1, 0, 2))[None],
        g_out[None], g_fc1[None], g_fc2.T[None], g_table.T[None], g_gain[None], g_shift[None],
    )


def solution(mesh):
    in_specs = (
        P("dp", "tensor", None),
        P("dp"),
        P(),
        P(),
        P("section", None, None, "tensor"),
        P("section", None, None, "tensor"),
        P("section", "tensor", None),
        P("section", None, "tensor"),
        P("section", "tensor", None),
        P("section", None, "tensor"),
        P("section", None, None),
        P("section", None, None),
        P("dp", "tensor", None),
    )
    out_specs = (
        P("dp", "tensor", None),
        P("section", "dp", "tensor", None),
        P("section", "dp", None, "tensor"),
        P("section", "dp", None, "tensor"),
        P("section", "tensor", "dp"),
        P("section", "dp", "tensor"),
        P("section", "tensor", "dp"),
        P("section", None, "tensor"),
        P("section", None, None),
        P("section", None, None),
    )
    return jax.shard_map(
        per_device, mesh=mesh, in_specs=in_specs, out_specs=out_specs, check_vma=False
    )
```

profile of v0, /device:TPU:9, one launch (start us, length us, event | category | flops | bytes accessed | tf_op | source)
XLA Modules:
  0.0 193.9 jit_solution(5625958694857599747)
XLA Ops:
  0.6 1.3 fusion
  5.8 0.8 constant_dynamic-slice_fusion.1
  6.6 0.6 pad_maximum_fusion.temb_hbm
  7.2 175.3 %blocks.1 = (bf16[2,64,1152]{2,1,0:T(8,128)(2,1)}, bf16[2,64,1152]{2,1,0:T(8,128)(2,1)}, bf16[16,128]{1,0:T(8,128)(2,1)}, f32[288,1152]{1,0:T(8,128)}, f32[288,1...) custom-call(bf16[2,64,1152]{2,1,0:T(8,128)(2,1)} %x_hbm.1, ...), custom_call_target="tpu_custom_call" | custom-call | tf_op jit(solution)/shard_map/blocks/pallas_call | solution.py:1228
  182.5 1.8 slice_bitcast_fusion.2
  184.3 0.0 copy-start.3
  184.3 0.0 copy-start.2
  184.3 0.0 copy-start.1
  184.3 3.5 %slice_bitcast_fusion = (f32[1,288,3,288]{3,1,2,0:T(8,128)}, f32[1,288,3,288]{3,1,2,0:T(8,128)}) fusion(f32[3,288,384]{2,1,0:T(8,128)} %get-tuple-element.23, f32[3,288,384]{2,1,0:T(8,128)} %get-tuple-element.22), kind=kLoop, calls=%fused_computation | loop fusion | bytes 3981312 | tf_op jit(solution)/shard_map/broadcast_in_dim | solution.py:1270
  187.8 0.0 copy-done.3
  187.8 0.7 copy.30
  188.5 0.0 copy-done.2
  188.5 0.7 copy.31
  189.3 0.0 copy-done.1
  189.3 0.0 copy-start
  189.3 1.1 copy.32
  190.3 0.7 copy-done
  191.1 0.0 copy-start.4
  191.1 0.0 copy-start.6
  191.1 0.0 copy-start.5
  191.1 1.1 copy.33
  192.1 0.0 copy-done.4
  192.1 0.6 copy.34
  192.7 0.0 copy-done.6
  192.7 0.6 copy.35
  193.3 0.0 copy-done.5
  193.3 0.6 copy.36
Async XLA Ops:
  184.3 3.5 %copy-start.3 = (bf16[2,64,1152]{2,1,0:T(8,128)(2,1)S(1)}, bf16[2,64,1152]{2,1,0:T(8,128)(2,1)}, u32[]{:S(2)}) copy-start(bf16[2,64,1152]{2,1,0:T(8,128)(2,1)} %get-tuple-element.46) | copy-start | bytes 884740
  184.3 4.3 %copy-start.2 = (bf16[2,64,1152]{2,1,0:T(8,128)(2,1)S(1)}, bf16[2,64,1152]{2,1,0:T(8,128)(2,1)}, u32[]{:S(2)}) copy-start(bf16[2,64,1152]{2,1,0:T(8,128)(2,1)} %get-tuple-element.21) | copy-start | bytes 884740
  184.3 5.0 %copy-start.1 = (f32[288,1152]{1,0:T(8,128)S(1)}, f32[288,1152]{1,0:T(8,128)}, u32[]{:S(2)}) copy-start(f32[288,1152]{1,0:T(8,128)} %get-tuple-element.25) | copy-start | bytes 3981316
  189.3 1.8 copy-start
  191.1 1.1 copy-start.4
  191.1 1.7 copy-start.6
  191.1 2.3 %copy-start.5 = (f32[2,1152]{1,0:T(2,128)S(1)}, f32[2,1152]{1,0:T(2,128)}, u32[]{:S(2)}) copy-start(f32[2,1152]{1,0:T(2,128)} %get-tuple-element.29) | copy-start | bytes 27652
where the time goes:
time: 194 us
  Pallas kernels  175 us (90%)
  local copies, waits for them, and re-layouts  13.5 us (7%)
  between operations  4.55 us (2%)
    pallas_call x1, Pallas kernels, run_block(): pl.pallas_call(functools.partial(block_kernel, dims), out_shape=out_shape...  175 us
    unnamed x21, local copies, waits for them, and re-layouts  6.11 us

commit v1 on v0

--- a/solution.py
+++ b/solution.py
@@ -72,12 +72,12 @@
 def block_kernel(
     cfg,
     x_hbm, cot_hbm, wq_hbm, wt_hbm, wo_hbm, w1_hbm, w2_hbm, temb_hbm, gain_hbm, shift_hbm, rel_hbm, tab_hbm,
-    out_hbm, ig_hbm, parts_ref, g2_hbm, g1_hbm, gq_hbm, go_hbm, gt_hbm, gtab_hbm, ggain_hbm, gshift_hbm,
-    temb_ref, gain_ref, shift_ref, rel_ref, tab_ref, out_ref, ig_ref, tot_ref, mlp_ref, stage, tok_ref, emb_ref,
+    out_hbm, ig_hbm, parts_ref, mlp_hbm, gq_hbm, go_hbm, gt_hbm, gtab_hbm, ggain_hbm, gshift_hbm,
+    temb_ref, gain_ref, shift_ref, rel_ref, tab_ref, out_ref, ig_ref, mlp_ref, exact, tok_ref, emb_ref,
     gtab_ref, small_ref, ggain_ref, gshift_ref,
-    wq_ref, wo_ref, w1_ref, w2_ref, tp_ref, tx_ref, chosen, tab, partial, sums, arrived,
+    wq_ref, wo_ref, w1_ref, w2_ref, tp_ref, tx_ref, order_ref, tab, partial, sums, arrived,
     tiny_s, small_r,
-    xin, mid, gath, keep, rcv_c, rcv_y, snd_c, snd_y, bias, prob, qkv, att, act, dgel,
+    xin, gath, keep, rcv_c, rcv_y, snd_c, snd_y, bias, prob, qkv, att, act, dgel,
     xhat, inv, ymid, dy1, dqkv, dtail, dh, acc, turned, line, far_att, dqkv2, dtail2, far_att2,
     load_s, store_s, ag_s, ag_r, rs_s, rs_r, sec_s, sec_r, ch_s, ch_r, fac_s, fac_r, li_s, li_r, ti_s, ti_r, sm_s, sm_r,
 ):
@@ -216,7 +216,7 @@
             device_id={"section": 1 - s}, device_id_type=MESH,
         )
 
-    mid_copy = sec_copy(0, mid, xin)
+    mid_copy = sec_copy(0, ig_ref, xin)
     grad_copy = sec_copy(1, ig_ref, xin)
     out_copy = sec_copy(2, out_ref, out_ref)
 
@@ -358,7 +358,7 @@
         def finish(slot, copy):
             copy.wait_recv()
             whole = sums[c, block(z), :].astype(F32) + arrived[slot, c].astype(F32)
-            tot_ref[:, c * wide : (c + 1) * wide] = whole.astype(BF16)
+            sums[c, block(z), :] = whole.astype(BF16)
 
         @pl.when(is_mate)
         def _():
@@ -566,6 +566,14 @@
         ag_start(ATT, i)
 
     lane = lax.broadcasted_iota(jnp.int32, (1, 2 * seq), 1)
+
+    def choose():
+        step = 128
+        for r in range(0, 4 * seq, step):
+            bucket = r + lax.broadcasted_iota(jnp.int32, (step, 4 * seq), 0)
+            partial[1, r : r + step, : 4 * seq] = jnp.where(
+                bucket == order_ref[:1, :], 1.0, 0.0
+            ).astype(BF16)
 
     def tables():
         valid = lane < (2 * grid - 1) * grid
@@ -580,13 +588,11 @@
             moved = pltpu.roll(slab[c : c + 1, :], grid - c, 1)
             before = jnp.where((lane % grid == grid - c) & valid, moved, before)
         order = jnp.concatenate([jnp.where(valid, slab[:1, :], none), before], axis=1)
-        step = 128
-        for r in range(0, chosen.shape[0], step):
-            bucket = r + lax.broadcasted_iota(jnp.int32, (step, 4 * seq), 0)
-            chosen[r : r + step, :] = jnp.where(bucket == order, 1.0, 0.0).astype(BF16)
+        order_ref[...] = jnp.broadcast_to(order, order_ref.shape)
+        choose()
         tab[...] = jnp.zeros_like(tab)
         tab[:heads, : tab_ref.shape[1]] = tab_ref[...]
-        found = add_thirds(mm(in_thirds(tab[...]), chosen[...]))
+        found = add_thirds(mm(in_thirds(tab[...]), partial[1, : 4 * seq, : 4 * seq]))
         after, before = found[:, : 2 * seq], found[:, 2 * seq :]
         for c in range(grid):
             low = pltpu.roll(after, c, 1) if c else after
@@ -700,7 +706,7 @@
 
         @pl.when(s == 0)
         def _():
-            mid[i] = y
+            ig_ref[i] = y
             mid_copy(i).start()
 
         @pl.when(s == 1)
@@ -883,6 +889,7 @@
         mlp_own()
         share_factor(0)
         share_factor(1)
+        choose()
 
     ig_store = pltpu.make_async_copy(ig_ref, ig_hbm, store_s.at[18])
     out_store = pltpu.make_async_copy(out_ref, out_hbm, store_s.at[19])
@@ -1013,6 +1020,7 @@
             return carry
 
         lax.fori_loop(0, blocks, whole, 0)
+        choose()
     stores = []
 
     def store(src, dst):
@@ -1021,9 +1029,8 @@
         stores.append(copy)
         return copy
 
-    mlp_stores = []
     if chained:
-        mlp_stores = [store(mlp_ref.at[0], g2_hbm), store(mlp_ref.at[1], g1_hbm)]
+        store(mlp_ref, mlp_hbm)
     over_ring(lambda j: tiny_copy(1, j).wait_recv())
 
     def add_slot(j, total):
@@ -1035,44 +1042,32 @@
         small_copy(1, j).start()
     tab[...] = jnp.zeros_like(tab)
     tab[:heads, :] = tiny_s[1, count : count + heads, : 4 * seq]
-    found = add_thirds(mm_nt(in_thirds(tab[...]), chosen[...]))
+    found = add_thirds(mm_nt(in_thirds(tab[...]), partial[1, : 4 * seq, : 4 * seq]))
     gtab_ref[...] = found[:heads, : gtab_ref.shape[1]]
     store(gtab_ref, gtab_hbm)
 
     over_ring(lambda j: tiny_copy(0, j).wait_recv())
     mine = width // ring
-    tall = gt_hbm.shape[1]
     rows_of_emb = emb_ref[...].reshape(ring * 8, width)
     rows_of_emb = pltpu.roll(rows_of_emb, (width - z * mine) % width, 1)[:, :mine].astype(BF16)
     right = in_thirds(tok_ref[...].reshape(ring * 8, width)[:, :lanes])
     over_images = mm_tn(jnp.concatenate([rows_of_emb] * 3, axis=0), right)
-    for copy in mlp_stores:
-        copy.wait()
-    room = mlp_ref.at[0] if chained else stage
     time_stores = []
     for c in range(3):
         first = c * local // 128 * 128
         window = over_images[:, first : first + wide]
         if c * local > first:
             window = pltpu.roll(window, wide - (c * local - first), 1)
-        room[:mine, c * wide : (c + 1) * wide] = window
-        time_stores.append(store(room.at[pl.ds(0, tall), pl.ds(c * wide, wide)], gt_hbm.at[c]))
+        exact[c, :mine, :] = window[:, :local]
+        time_stores.append(store(exact.at[c], gt_hbm.at[c]))
     if chained:
-        for c in (full, *range(full)):
-            settle(c)
-        for c in range(3):
-            first = c * local // 128 * 128
-            window = tot_ref[:, first : first + wide].astype(F32)
-            if c * local > first:
-                window = pltpu.roll(window, wide - (c * local - first), 1)
-            mlp_ref[1, :, c * wide : (c + 1) * wide] = window
-            store(mlp_ref.at[1, :, pl.ds(c * wide, wide)], gq_hbm.at[c])
-        window = tot_ref[:, width - wide :].astype(F32)
+        settle(full)
+        window = sums[full, block(z), :].astype(F32)
         window = pltpu.roll(window, wide - (3 * local - (width - wide)), 1)
         for copy in time_stores:
             copy.wait()
-        mlp_ref[0, :, :wide] = wider(window.T[:local], wide)
-        store(mlp_ref.at[0, :, pl.ds(0, wide)], go_hbm)
+        exact[0] = window.T[:local]
+        out_grad_store = store(exact.at[0], go_hbm)
     for j in range(3):
         small_copy(1, j).wait_recv()
     last = count + heads
@@ -1083,6 +1078,24 @@
     gshift_ref[...] = small_ref[2:, :]
     store(ggain_ref, ggain_hbm)
     store(gshift_ref, gshift_hbm)
+    if chained:
+        settled = 0
+        for c in range(3):
+            first = c * local // 128 * 128
+            while settled < full and settled * wide < first + wide:
+                settle(settled)
+                settled += 1
+            n, offset = first // wide, first % wide
+            window = sums[n, block(z), offset:]
+            if offset:
+                window = jnp.concatenate([window, sums[n + 1, block(z), :offset]], axis=1)
+            window = window.astype(F32)
+            if c * local > first:
+                window = pltpu.roll(window, wide - (c * local - first), 1)
+            if c == 0:
+                out_grad_store.wait()
+            exact[c] = window[:, :local]
+            store(exact.at[c], gq_hbm.at[c])
 
     def finish(i):
         for k in (MLP, DMLP, DATT):
@@ -1108,7 +1121,7 @@
         small_copy(1, j).wait_send()
     if chained:
         weights_left()
-    waited = mlp_stores + (time_stores if chained else [])
+    waited = time_stores + [out_grad_store] if chained else []
     for copy in stores:
         if all(copy is not done for done in waited):
             copy.wait()
@@ -1120,7 +1133,7 @@
     heads = table.shape[0]
     local = wo.shape[0]
     hidden = w1.shape[1]
-    chained = ring == 4 and count == 2 and width % (16 * ring) == 0
+    chained = ring == 4 and count == 2 and width % (16 * ring) == 0 and local == width // ring
     blocks = 4
     pieces = 3 if width // 4 % 48 == 0 else 1
     cut = width // blocks
@@ -1135,11 +1148,10 @@
         jax.ShapeDtypeStruct((count, rows, width), BF16),
         jax.ShapeDtypeStruct((count, rows, width), BF16),
         jax.ShapeDtypeStruct((16, 128) if chained else (3, blocks, cut, width), BF16),
-        jax.ShapeDtypeStruct((cut, width) if chained else small, F32),
-        jax.ShapeDtypeStruct((cut, width) if chained else small, F32),
-        jax.ShapeDtypeStruct((3, cut, padded) if chained else small, F32),
-        jax.ShapeDtypeStruct((local, padded) if chained else small, F32),
-        jax.ShapeDtypeStruct((3, -(-mine // 8) * 8, padded), F32),
+        jax.ShapeDtypeStruct((2, cut, width) if chained else small, F32),
+        jax.ShapeDtypeStruct((3, cut, local) if chained else small, F32),
+        jax.ShapeDtypeStruct((local, cut) if chained else small, F32),
+        jax.ShapeDtypeStruct((3, -(-mine // 8) * 8, local), F32),
         jax.ShapeDtypeStruct(table.shape, F32),
         jax.ShapeDtypeStruct((2, width), F32),
         jax.ShapeDtypeStruct((2, width), F32),
@@ -1154,9 +1166,8 @@
         vm(table.shape, F32),
         vm((count, rows, width), BF16),
         vm((count, rows, width), BF16),
-        vm((cut, width) if chained else (16, 128), BF16),
         vm((2, cut, width) if chained else (2, 8, 128), F32),
-        vm(small if chained else (-(-mine // 8) * 8, 3 * padded), F32),
+        vm((3, -(-mine // 8) * 8, local), F32),
         vm((ring, 8, width), F32),
         vm((ring, 8, width), F32),
         vm(table.shape, F32),
@@ -1169,14 +1180,13 @@
         vm(w2.shape, BF16),
         vm((3, 16, local), F32),
         vm((heads, int(round(seq**0.5)), 2 * seq), F32),
-        vm((4 * seq, 4 * seq), BF16),
+        vm((8, 4 * seq), jnp.int32),
         vm((16, 4 * seq), F32),
         vm((2, width, width), BF16),
         vm((pieces, width, padded), BF16),
         vm((2, pieces, cut, padded) if chained else (16, 128), BF16),
         vm((2, 8, width), F32),
         vm((2, 3, 8, width), F32),
-        vm((count, rows, width), BF16),
         vm((count, rows, width), BF16),
         vm((3, count, seq, width), BF16),
         vm((2, count, 2, rows, width), F32),
@@ -1229,7 +1239,7 @@
         functools.partial(block_kernel, dims),
         out_shape=out_shape,
         in_specs=[lies] * 12,
-        out_specs=[lies] * 2 + [lies if chained else whole] + [lies] * 8,
+        out_specs=[lies] * 2 + [lies if chained else whole] + [lies] * 7,
         scratch_shapes=scratch,
         compiler_params=pltpu.CompilerParams(
             collective_id=0, has_side_effects=True, vmem_limit_bytes=63 * 2**20
@@ -1247,12 +1257,13 @@
     width = images.shape[-1]
     local = w_out.shape[1]
     cut = width // ring
-    embedded = jnp.concatenate(
-        [lax.dynamic_slice_in_dim(t_table, timesteps[i], 1, axis=0) for i in range(count)], axis=0
-    )
+    steps = lax.broadcasted_iota(jnp.int32, (count, t_table.shape[0]), 1)
+    embedded = jnp.dot(
+        (steps == timesteps[:, None]).astype(BF16), t_table, preferred_element_type=F32
+    ).astype(BF16)
     wq = jnp.transpose(w_qkv[0], (1, 2, 0)).reshape(3 * local, width)
     wt = jnp.transpose(w_time[0], (1, 2, 0)).reshape(3 * local, width)
-    output, in_grad, parts, g_fc2, g_fc1, g_qkv, g_out, g_time, g_table, g_gain, g_shift = run_block(
+    output, in_grad, parts, mlp, g_qkv, g_out, g_time, g_table, g_gain, g_shift = run_block(
         images, cotangent, wq, wt, w_out[0], w_fc1[0], w_fc2[0], embedded, norm_gain[0], norm_shift[0],
         rel_index, rel_table[0].T, ring,
     )
@@ -1264,11 +1275,12 @@
         g_qkv = jnp.transpose(rest[:, : 3 * local].reshape(cut, 3, local), (1, 0, 2))
         g_out = rest[:, 3 * local :].T
     else:
-        g_qkv, g_out = g_qkv[:, :, :local], g_out[:, :cut]
-    g_time = g_time[:, : width // ring, :local]
+        g_fc2, g_fc1 = mlp
+    g_time = g_time[:, : width // ring]
     return (
-        output, in_grad[None], jnp.transpose(g_qkv, (1, 0, 2))[None], jnp.transpose(g_time, (1, 0, 2))[None],
-        g_out[None], g_fc1[None], g_fc2.T[None], g_table.T[None], g_gain[None], g_shift[None],
+        output, in_grad[None], jnp.transpose(g_qkv, (1, 0, 2))[None],
+        jnp.transpose(g_time, (1, 0, 2))[None], g_out[None], g_fc1[None], g_fc2.T[None],
+        g_table.T[None], g_gain[None], g_shift[None],
     )
 
 

time: 194 us -> 189 us (0.974)
  between operations: 4.55 us -> 0.69 us
  local copies, waits for them, and re-layouts: 13.5 us -> 9.67 us
  matrix products: 0 us -> 2.72 us
    dot_general x0 -> x1, matrix products: none -> 2.72 us  [per_device(): jnp.dot((steps == timesteps[:, None]).astype(BF16), t_table, preferred_el...]
    broadcast_in_dim x2 -> x1, local copies, waits for them, and re-layouts: 5.33 us -> 3.53 us  [per_device(): g_fc2.T[None]]
    unnamed x21 -> x24, local copies, waits for them, and re-layouts: 6.11 us -> 6.15 us
where the time goes in v1:
time: 189 us
  Pallas kernels  176 us (93%)
  local copies, waits for them, and re-layouts  9.67 us (5%)
  matrix products  2.72 us (1%)
    pallas_call x1, Pallas kernels, run_block(): pl.pallas_call(functools.partial(block_kernel, dims), out_shape=out_shape...  176 us
    unnamed x24, local copies, waits for them, and re-layouts  6.15 us

profile of v1, /device:TPU:9, one launch (start us, length us, event | category | flops | bytes accessed | tf_op | source)
XLA Modules:
  0.0 188.7 jit_solution(8979691479137846445)
XLA Ops:
  0.6 2.7 %convolution_convert_fusion.temb_hbm = bf16[2,1152]{1,0:T(2,128)(2,1)} fusion(bf16[1000,1152]{1,0:T(8,128)(2,1)} %param.15, s32[2]{0:T(128)} %param.14), kind=kOutput, calls=%fused_computation | convolution fusion | flops 4612304 | bytes 2308616 | tf_op jit(solution)/shard_map/dot_general | solution.py:1261
  3.4 175.7 %blocks.1 = (bf16[2,64,1152]{2,1,0:T(8,128)(2,1)}, bf16[2,64,1152]{2,1,0:T(8,128)(2,1)}, bf16[16,128]{1,0:T(8,128)(2,1)}, f32[2,288,1152]{2,1,0:T(8,128)}, f32[3...) custom-call(bf16[2,64,1152]{2,1,0:T(8,128)(2,1)} %x_hbm.1, ...), custom_call_target="tpu_custom_call" | custom-call | tf_op jit(solution)/shard_map/blocks/pallas_call | solution.py:1238
  179.0 0.0 copy-start.4
  179.0 0.0 copy-start.3
  179.1 0.0 copy-start.1
  179.1 3.5 %slice_bitcast_fusion = (f32[1,1152,288]{1,2,0:T(8,128)}, f32[1,288,1152]{2,1,0:T(8,128)}) fusion(f32[2,288,1152]{2,1,0:T(8,128)} %get-tuple-element.24), kind=kLoop, calls=%fused_computation.1 | loop fusion | bytes 5308416 | tf_op jit(solution)/shard_map/broadcast_in_dim | solution.py:1282
  182.6 0.0 copy-start
  182.6 0.0 copy-done.4
  182.6 0.7 copy.31
  183.3 0.0 copy-done.3
  183.3 0.7 copy.32
  184.0 0.0 copy-done.1
  184.0 0.0 copy-start.2
  184.0 1.1 copy.33
  185.1 0.0 copy-done
  185.1 0.0 copy-start.5
  185.1 0.0 copy-start.7
  185.1 0.0 copy-start.6
  185.1 1.1 copy.34
  186.2 0.0 copy-done.2
  186.2 0.8 copy.35
  186.9 0.0 copy-done.5
  186.9 0.6 copy.36
  187.5 0.0 copy-done.7
  187.5 0.6 copy.37
  188.1 0.0 copy-done.6
  188.1 0.6 copy.38
Async XLA Ops:
  179.0 3.6 %copy-start.4 = (bf16[2,64,1152]{2,1,0:T(8,128)(2,1)S(1)}, bf16[2,64,1152]{2,1,0:T(8,128)(2,1)}, u32[]{:S(2)}) copy-start(bf16[2,64,1152]{2,1,0:T(8,128)(2,1)} %get-tuple-element.40) | copy-start | bytes 884740
  179.0 4.3 %copy-start.3 = (bf16[2,64,1152]{2,1,0:T(8,128)(2,1)S(1)}, bf16[2,64,1152]{2,1,0:T(8,128)(2,1)}, u32[]{:S(2)}) copy-start(bf16[2,64,1152]{2,1,0:T(8,128)(2,1)} %get-tuple-element.20) | copy-start | bytes 884740
  179.1 5.0 %copy-start.1 = (f32[3,288,288]{2,1,0:T(8,128)S(1)}, f32[3,288,288]{2,1,0:T(8,128)}, u32[]{:S(2)}) copy-start(f32[3,288,288]{2,1,0:T(8,128)} %get-tuple-element.21) | copy-start | bytes 2985988
  182.6 2.5 %copy-start = (f32[3,288,288]{2,1,0:T(8,128)S(1)}, f32[3,288,288]{2,1,0:T(8,128)}, u32[]{:S(2)}) copy-start(f32[3,288,288]{2,1,0:T(8,128)} %get-tuple-element.22) | copy-start | bytes 2985988
  184.0 2.1 %copy-start.2 = (f32[288,288]{1,0:T(8,128)S(1)}, f32[288,288]{1,0:T(8,128)}, u32[]{:S(2)}) copy-start(f32[288,288]{1,0:T(8,128)} %get-tuple-element.23) | copy-start | bytes 995332
  185.1 1.8 copy-start.5
  185.1 2.4 %copy-start.7 = (f32[2,1152]{1,0:T(2,128)S(1)}, f32[2,1152]{1,0:T(2,128)}, u32[]{:S(2)}) copy-start(f32[2,1152]{1,0:T(2,128)} %get-tuple-element.26) | copy-start | bytes 27652
  185.1 3.0 %copy-start.6 = (f32[2,1152]{1,0:T(2,128)S(1)}, f32[2,1152]{1,0:T(2,128)}, u32[]{:S(2)}) copy-start(f32[2,1152]{1,0:T(2,128)} %get-tuple-element.27) | copy-start | bytes 27652

commit v2 on v1

--- a/solution.py
+++ b/solution.py
@@ -251,9 +251,11 @@
     def block(b):
         return pl.ds(pl.multiple_of(b * cut, cut), cut)
 
+    mate_rows = pl.ds(pl.multiple_of((1 - z // 2) * cut, cut), 3 * cut)
+
     def factor_copy(n):
         if n < 2:
-            src, dst = turned.at[n, t % 2], turned.at[n, count + t % 2]
+            src, dst = turned.at[n, t % 2, mate_rows, :], turned.at[n, count + t % 2, mate_rows, :]
         else:
             pairs = [(dqkv.at[c], dqkv2.at[c]) for c in range(full)] + [(dtail, dtail2), (far_att, far_att2)]
             src, dst = pairs[n - 2]
@@ -263,7 +265,7 @@
         )
 
     def share_copy(k):
-        ref = turned.at[k, count + t % 2]
+        ref = turned.at[k, count + t % 2, mate_rows, :]
         return pltpu.make_async_remote_copy(
             src_ref=ref, dst_ref=ref, send_sem=fac_s.at[4 + full + k], recv_sem=fac_r.at[4 + full + k],
             device_id={"tensor": core}, device_id_type=MESH,

time: 189 us -> 186 us (0.984)
  Pallas kernels: 176 us -> 173 us
    pallas_call x1, Pallas kernels: 176 us -> 173 us  [run_block(): pl.pallas_call(functools.partial(block_kernel, dims), out_shape=out_shape...]
where the time goes in v2:
time: 186 us
  Pallas kernels  173 us (93%)
  local copies, waits for them, and re-layouts  9.67 us (5%)
  matrix products  2.72 us (1%)
    pallas_call x1, Pallas kernels, run_block(): pl.pallas_call(functools.partial(block_kernel, dims), out_shape=out_shape...  173 us
    unnamed x24, local copies, waits for them, and re-layouts  6.15 us

profile of v2, /device:TPU:9, one launch (start us, length us, event | category | flops | bytes accessed | tf_op | source)
XLA Modules:
  0.0 186.1 jit_solution(5733326730019123250)
XLA Ops:
  0.6 2.7 %convolution_convert_fusion.temb_hbm = bf16[2,1152]{1,0:T(2,128)(2,1)} fusion(bf16[1000,1152]{1,0:T(8,128)(2,1)} %param.15, s32[2]{0:T(128)} %param.14), kind=kOutput, calls=%fused_computation | convolution fusion | flops 4612304 | bytes 2308616 | tf_op jit(solution)/shard_map/dot_general | solution.py:1263
  3.4 173.0 %blocks.1 = (bf16[2,64,1152]{2,1,0:T(8,128)(2,1)}, bf16[2,64,1152]{2,1,0:T(8,128)(2,1)}, bf16[16,128]{1,0:T(8,128)(2,1)}, f32[2,288,1152]{2,1,0:T(8,128)}, f32[3...) custom-call(bf16[2,64,1152]{2,1,0:T(8,128)(2,1)} %x_hbm.1, ...), custom_call_target="tpu_custom_call" | custom-call | tf_op jit(solution)/shard_map/blocks/pallas_call | solution.py:1240
  176.4 0.0 copy-start.4
  176.4 0.0 copy-start.3
  176.4 0.0 copy-start.1
  176.4 3.5 %slice_bitcast_fusion = (f32[1,1152,288]{1,2,0:T(8,128)}, f32[1,288,1152]{2,1,0:T(8,128)}) fusion(f32[2,288,1152]{2,1,0:T(8,128)} %get-tuple-element.24), kind=kLoop, calls=%fused_computation.1 | loop fusion | bytes 5308416 | tf_op jit(solution)/shard_map/broadcast_in_dim | solution.py:1284
  179.9 0.0 copy-start
  179.9 0.0 copy-done.4
  179.9 0.7 copy.31
  180.7 0.0 copy-done.3
  180.7 0.7 copy.32
  181.4 0.0 copy-done.1
  181.4 0.0 copy-start.2
  181.4 1.1 copy.33
  182.4 0.0 copy-done
  182.4 0.0 copy-start.5
  182.4 0.0 copy-start.7
  182.4 0.0 copy-start.6
  182.4 1.1 copy.34
  183.5 0.0 copy-done.2
  183.5 0.8 copy.35
  184.3 0.0 copy-done.5
  184.3 0.6 copy.36
  184.9 0.0 copy-done.7
  184.9 0.6 copy.37
  185.5 0.0 copy-done.6
  185.5 0.6 copy.38
Async XLA Ops:
  176.4 3.6 %copy-start.4 = (bf16[2,64,1152]{2,1,0:T(8,128)(2,1)S(1)}, bf16[2,64,1152]{2,1,0:T(8,128)(2,1)}, u32[]{:S(2)}) copy-start(bf16[2,64,1152]{2,1,0:T(8,128)(2,1)} %get-tuple-element.40) | copy-start | bytes 884740
  176.4 4.3 %copy-start.3 = (bf16[2,64,1152]{2,1,0:T(8,128)(2,1)S(1)}, bf16[2,64,1152]{2,1,0:T(8,128)(2,1)}, u32[]{:S(2)}) copy-start(bf16[2,64,1152]{2,1,0:T(8,128)(2,1)} %get-tuple-element.20) | copy-start | bytes 884740
  176.4 5.0 %copy-start.1 = (f32[3,288,288]{2,1,0:T(8,128)S(1)}, f32[3,288,288]{2,1,0:T(8,128)}, u32[]{:S(2)}) copy-start(f32[3,288,288]{2,1,0:T(8,128)} %get-tuple-element.21) | copy-start | bytes 2985988
  179.9 2.5 %copy-start = (f32[3,288,288]{2,1,0:T(8,128)S(1)}, f32[3,288,288]{2,1,0:T(8,128)}, u32[]{:S(2)}) copy-start(f32[3,288,288]{2,1,0:T(8,128)} %get-tuple-element.22) | copy-start | bytes 2985988
  181.4 2.1 %copy-start.2 = (f32[288,288]{1,0:T(8,128)S(1)}, f32[288,288]{1,0:T(8,128)}, u32[]{:S(2)}) copy-start(f32[288,288]{1,0:T(8,128)} %get-tuple-element.23) | copy-start | bytes 995332
  182.4 1.8 copy-start.5
  182.4 2.4 %copy-start.7 = (f32[2,1152]{1,0:T(2,128)S(1)}, f32[2,1152]{1,0:T(2,128)}, u32[]{:S(2)}) copy-start(f32[2,1152]{1,0:T(2,128)} %get-tuple-element.26) | copy-start | bytes 27652
  182.4 3.0 %copy-start.6 = (f32[2,1152]{1,0:T(2,128)S(1)}, f32[2,1152]{1,0:T(2,128)}, u32[]{:S(2)}) copy-start(f32[2,1152]{1,0:T(2,128)} %get-tuple-element.27) | copy-start | bytes 27652
